TPU v7x, 32 devices: a whole 2x2x4 slice. The times are simulated.
32 devices in a mesh: row: 4 (over z), col: 8 (over y, x, core).
Axes of the slice: x: 2, y: 2, z: 4, core: 2. Of those that a mesh axis runs over, the one named last changes fastest.
Arguments:
- amplitudes: float32 [1024, 131072], P('col', 'row'), may hold values from -6 to 6
- integrals: float32 [131072, 3072], P(('row', 'col')), may hold values from -0.03125 to 0.03125
Outputs:
- ladder: float32 [1024, 3072], P('col', 'row')
All inputs are finite; a program needn't handle non-finite values.
Results may differ from a plain program's by a relative error of at most 0.00011.
Values sent between devices are 32-bit elements; how exact they have to be, the bound alone decides.
A program may use at most 192 MiB of HBM per device.

v0:
```python
import jax
import jax.numpy as jnp
from jax import lax
from jax.sharding import PartitionSpec as P


def body(amplitudes, integrals):
    received = lax.all_to_all(amplitudes, "col", split_axis=1, concat_axis=0, tiled=True)
    by_pair = lax.psum_scatter(
        jnp.dot(
            received, integrals, precision=lax.Precision.HIGHEST, preferred_element_type=jnp.float32
        ),
        "col",
        scatter_dimension=0,
        tiled=True,
    )
    ladder = 0.5 * lax.psum_scatter(by_pair, "row", scatter_dimension=1, tiled=True)
    return ladder


def solution(mesh):
    return jax.shard_map(
        body,
        mesh=mesh,
        in_specs=(P("col", "row"), P(("row", "col"), None)),
        out_specs=P("col", "row"),
        check_vma=False,
    )
```

profile of v0, /device:TPU:0, one launch (start us, length us, event | category | flops | bytes accessed | tf_op | source)
XLA Modules:
  0.0 538.9 jit_solution(11794522305320470507)
XLA Ops:
  6.5 0.0 reduce-scatter.3.cloned.1.call-start
  6.5 17.4 %copy.3 = f32[128,32768]{0,1:T(8,128)} copy(f32[128,32768]{1,0:T(8,128)} %param.2) | data formatting | bytes 33554432 | tf_op args[0]
  23.9 192.1 %all_to_all.19 = f32[128,8,4096]{0,2,1:T(8,128)} all-to-all(f32[128,8,4096]{0,2,1:T(8,128)} %bitcast.6), channel_id=1, replica_groups=mesh['row'=4,'col'=8] {'col'}, dimensions={1} | all-to-all | bytes 33554432 | tf_op jit(solution)/shard_map/all_to_all | solution.py:8
  216.1 17.5 %copy.4 = f32[8,128,4096]{2,1,0:T(8,128)} copy(f32[8,128,4096]{1,2,0:T(8,128)} %bitcast.5) | data formatting | bytes 33554432 | tf_op jit(solution)/shard_map/all_to_all | solution.py:8
  233.6 166.4 %fusion = f32[1024,3072]{1,0:T(8,128)} fusion(f32[1024,4096]{1,0:T(8,128)} %bitcast.7, f32[4096,3072]{1,0:T(8,128)} %param.3), kind=kOutput, calls=%fused_computation.1 | convolution fusion | flops 154618822656 | bytes 79691776 | tf_op jit(solution)/shard_map/dot_general | solution.py:10
  400.0 0.0 reduce-scatter.3.cloned.1.call-update
  400.0 0.0 reduce-scatter.5.cloned.1.call-start
  400.1 92.6 %reduce-scatter.3.cloned.1.call-done = f32[128,3072]{1,0:T(8,128)} async-done(((f32[1024,3072]{1,0:T(8,128)}), f32[128,3072]{1,0:T(8,128)}) %reduce-scatter.3.cloned.1.call-update) | async-done | bytes 1572880 | tf_op jit(solution)/shard_map/reduce_scatter | solution.py:9
  492.7 0.0 reduce-scatter.5.cloned.1.call-update
  492.7 37.6 %reduce-scatter.5.cloned.1.call-done = f32[128,768]{1,0:T(8,128)} async-done(((f32[128,3072]{1,0:T(8,128)}), f32[128,768]{1,0:T(8,128)}) %reduce-scatter.5.cloned.1.call-update) | async-done | bytes 393232 | tf_op jit(solution)/shard_map/reduce_scatter | solution.py:17
  530.3 1.8 broadcast_multiply_fusion
Async XLA Ops:
  6.5 486.1 %reduce-scatter.3.cloned.1.call-start = ((), (), s32[]{:S(2)}) async-start(), calls=%async_computation.3 | async-start | bytes 14155776 | tf_op jit(solution)/shard_map/reduce_scatter | solution.py:9
  400.0 130.3 %reduce-scatter.5.cloned.1.call-start = ((), (), s32[]{:S(2)}) async-start(), calls=%async_computation.4 | async-start | bytes 1966080 | tf_op jit(solution)/shard_map/reduce_scatter | solution.py:17
Sparse Core Ops, SparseCore 0:
  400.1 92.4 reduce-scatter.2
  495.0 35.2 reduce-scatter.4
where the time goes:
time: 540 us; the launch traced here: 539 us
  blocking collectives  192 us (36%)
  matrix products  166 us (31%)
  waiting for transfers between devices  130 us (24%)
  local copies, waits for them, and re-layouts  34.9 us (6%)
  between operations  13.4 us (2%)
    all_to_all x1, blocking collectives, body(): lax.all_to_all(amplitudes, 'col', split_axis=1, concat_axis=0, tiled=True)  192 us
    dot_general x1, matrix products, body(): jnp.dot(received, integrals, precision=lax.Precision.HIGHEST, preferred_e...  166 us
    reduce_scatter x1, waiting for transfers between devices, body(): lax.psum_scatter(jnp.dot(received, integrals, precision=lax.Precision.HIG...  92.6 us
    reduce_scatter x1, waiting for transfers between devices, body(): lax.psum_scatter(by_pair, 'row', scatter_dimension=1, tiled=True)  37.6 us
    all_to_all x1, local copies, waits for them, and re-layouts, body(): lax.all_to_all(amplitudes, 'col', split_axis=1, concat_axis=0, tiled=True)  17.5 us
    unnamed x1, local copies, waits for them, and re-layouts  17.4 us
  transfers between devices with their start and end apart: 2, of which 2 were waited for; matrix products, arithmetic and copies ran while one was open for 0% of the time, Pallas kernels for 0%

commit v1 on v0

v1 whole, which is shorter than its diff:
```python
import functools

import jax
import jax.numpy as jnp
from jax import lax
from jax.experimental import pallas as pl
from jax.experimental.pallas import tpu as pltpu
from jax.sharding import PartitionSpec as P

MESH = pl.DeviceIdType.MESH
BF16, F32 = jnp.bfloat16, jnp.float32
SLOTS = 3
CHUNKS = 4


def kernel(
    rows, cols, m, chunks, depth, tn, kt,
    a, b, out,
    recv, xhi, xlo, bbuf, acc, part, pair_in, z_in, plane, plane_in,
    own_sem, a_send, a_recv, b_sem, p_send, p_recv, z_send, z_recv, q_send, q_recv,
):
    r, c = lax.axis_index("row"), lax.axis_index("col")
    chips = cols // 2
    core, chip = lax.rem(c, 2), lax.div(c, 2)
    sibling = c + 1 - 2 * core
    half = chips * m
    slab = out.shape[1]
    per = slab // tn
    tiles = rows * per

    def place(col):
        return pl.multiple_of((lax.rem(col, 2) * chips + lax.div(col, 2)) * m, 8)

    def own_copy(s):
        return pltpu.make_async_copy(
            a.at[pl.ds(pl.multiple_of(s * m, 8), m), pl.ds(pl.multiple_of(c * depth, 128), depth)],
            recv.at[s, pl.ds(place(c), m)],
            own_sem.at[s],
        )

    def a_copy(s, k, slot_of):
        peer = lax.rem(c + k, cols)
        return pltpu.make_async_remote_copy(
            src_ref=a.at[
                pl.ds(pl.multiple_of(s * m, 8), m), pl.ds(pl.multiple_of(peer * depth, 128), depth)
            ],
            dst_ref=recv.at[s, pl.ds(place(slot_of), m)],
            send_sem=a_send.at[s, k - 1],
            recv_sem=a_recv.at[s, k - 1],
            device_id={"col": peer},
            device_id_type=MESH,
        )

    def b_copy(t):
        j = lax.rem(t, tiles)
        rr = lax.rem(r + 1 + lax.div(j, per), rows)
        col = rr * slab + lax.rem(j, per) * tn
        return pltpu.make_async_copy(
            b.at[:, pl.ds(pl.multiple_of(col, 128), tn)],
            bbuf.at[lax.rem(t, SLOTS)],
            b_sem.at[lax.rem(t, SLOTS)],
        )

    def pair_copy(s, jr):
        rr = lax.rem(r + 1 + jr, rows)
        return pltpu.make_async_remote_copy(
            src_ref=part.at[lax.rem(s, 2), 1 - core, rr],
            dst_ref=pair_in.at[s, jr],
            send_sem=p_send.at[s, jr],
            recv_sem=p_recv.at[s, jr],
            device_id={"col": sibling},
            device_id_type=MESH,
        )

    def z_copy(s, jr):
        rr = lax.rem(r + 1 + jr, rows)
        return pltpu.make_async_remote_copy(
            src_ref=part.at[lax.rem(s, 2), core, rr],
            dst_ref=z_in.at[s, jr],
            send_sem=z_send.at[s, jr],
            recv_sem=z_recv.at[s, jr],
            device_id={"row": rr},
            device_id_type=MESH,
        )

    def plane_copy(s, k):
        there = lax.rem(chip + k, chips)
        return pltpu.make_async_remote_copy(
            src_ref=plane.at[s, pl.ds(pl.multiple_of(there * m, 8), m)],
            dst_ref=plane_in.at[s, k - 1],
            send_sem=q_send.at[s, k - 1],
            recv_sem=q_recv.at[s, k - 1],
            device_id={"col": 2 * there + core},
            device_id_type=MESH,
        )

    def pair_finish(s, jr):
        rr = lax.rem(r + 1 + jr, rows)
        copy = pair_copy(s, jr)
        copy.wait_recv()
        copy.wait_send()
        now = lax.rem(s, 2)
        part[now, core, rr] = part[now, core, rr] + pair_in[s, jr]

    def z_finish(s):
        @pl.loop(0, rows - 1)
        def _(k):
            copy = z_copy(s, k)
            copy.wait_recv()
            copy.wait_send()

        total = part[lax.rem(s, 2), core, r]
        for k in range(rows - 1):
            total = total + z_in[s, k]
        plane[s] = total

        @pl.loop(1, chips)
        def _(k):
            plane_copy(s, k).start()

    def plane_finish(s):
        @pl.loop(1, chips)
        def _(k):
            copy = plane_copy(s, k)
            copy.wait_recv()
            copy.wait_send()

        total = plane[s, pl.ds(pl.multiple_of(chip * m, 8), m)]
        for k in range(chips - 1):
            total = total + plane_in[s, k]
        out[pl.ds(pl.multiple_of(s * m, 8), m), :] = 0.5 * total

    def tile(s, jr, jt):
        rr = lax.rem(r + 1 + jr, rows)
        t = s * tiles + jr * per + jt
        b_copy(t).wait()

        @pl.when(t + SLOTS - 1 < chunks * tiles)
        def _():
            b_copy(t + SLOTS - 1).start()

        slot = lax.rem(t, SLOTS)
        acc[...] = jnp.zeros_like(acc)

        @pl.loop(0, depth // kt)
        def _(kk):
            at = pl.ds(pl.multiple_of(kk * kt, 128), kt)
            block = bbuf[slot, at, :]
            bh = block.astype(BF16)
            bl = (block - bh.astype(F32)).astype(BF16)
            xh, xl = xhi[:, at], xlo[:, at]
            acc[...] += (
                jnp.dot(xh, bh, preferred_element_type=F32)
                + jnp.dot(xl, bh, preferred_element_type=F32)
                + jnp.dot(xh, bl, preferred_element_type=F32)
            )

        now = lax.rem(s, 2)
        at = pl.ds(pl.multiple_of(jt * tn, 128), tn)
        part[now, 0, rr, :, at] = acc[:half]
        part[now, 1, rr, :, at] = acc[half:]

    for t in range(SLOTS - 1):
        b_copy(jnp.int32(t)).start()

    barrier = pltpu.get_barrier_semaphore()

    @pl.loop(1, cols)
    def _(k):
        pl.semaphore_signal(
            barrier, inc=1, device_id={"col": lax.rem(c + k, cols)}, device_id_type=MESH
        )

    @pl.loop(1, rows)
    def _(k):
        pl.semaphore_signal(
            barrier, inc=1, device_id={"row": lax.rem(r + k, rows)}, device_id_type=MESH
        )

    pl.semaphore_wait(barrier, cols - 1 + rows - 1)

    @pl.loop(1, cols)
    def _(k):
        a_copy(0, k, c).start()

    own_copy(0).start()

    @pl.loop(0, chunks)
    def _(s):
        @pl.loop(1, cols)
        def _(k):
            a_copy(s, k, c).wait_send()

            @pl.when(s + 1 < chunks)
            def _():
                a_copy(s + 1, k, c).start()

        own_copy(s).wait()

        @pl.when(s + 1 < chunks)
        def _():
            own_copy(s + 1).start()

        @pl.loop(1, cols)
        def _(k):
            a_copy(s, k, lax.rem(c - k + cols, cols)).wait_recv()

        @pl.loop(0, depth // kt)
        def _(kk):
            at = pl.ds(pl.multiple_of(kk * kt, 128), kt)
            block = recv[s, :, at]
            high = block.astype(BF16)
            xhi[:, at] = high
            xlo[:, at] = (block - high.astype(F32)).astype(BF16)

        @pl.loop(0, rows)
        def _(jr):
            @pl.loop(0, per)
            def _(jt):
                tile(s, jr, jt)

            pair_copy(s, jr).start()

            @pl.when(jr > 0)
            def _():
                pair_finish(s, jr - 1)
                z_copy(s, jr - 1).start()

        pair_finish(s, rows - 1)

        @pl.when(s > 0)
        def _():
            z_finish(s - 1)

        @pl.when(s > 1)
        def _():
            plane_finish(s - 2)

    z_finish(chunks - 1)
    plane_finish(chunks - 2)
    plane_finish(chunks - 1)


def body(rows, cols, amplitudes, integrals):
    occupied = amplitudes.shape[0]
    depth, width = integrals.shape
    m = max(8, occupied // CHUNKS)
    chunks = occupied // m
    slab = width // rows
    tn = 256 if slab % 256 == 0 else 128
    kt = min(512, depth)
    chips = cols // 2
    half = chips * m
    dma = pltpu.SemaphoreType.DMA
    vmem = pltpu.VMEM
    return pl.pallas_call(
        functools.partial(kernel, rows, cols, m, chunks, depth, tn, kt),
        out_shape=jax.ShapeDtypeStruct((occupied, slab), F32),
        in_specs=[pl.BlockSpec(memory_space=pl.ANY)] * 2,
        out_specs=pl.BlockSpec(memory_space=vmem),
        scratch_shapes=[
            vmem((chunks, cols * m, depth), F32),
            vmem((cols * m, depth), BF16),
            vmem((cols * m, depth), BF16),
            vmem((SLOTS, depth, tn), F32),
            vmem((cols * m, tn), F32),
            vmem((2, 2, rows, half, slab), F32),
            vmem((chunks, rows, half, slab), F32),
            vmem((chunks, rows - 1, half, slab), F32),
            vmem((chunks, half, slab), F32),
            vmem((chunks, chips - 1, m, slab), F32),
            dma((chunks,)),
            dma((chunks, cols - 1)),
            dma((chunks, cols - 1)),
            dma((SLOTS,)),
            dma((chunks, rows)),
            dma((chunks, rows)),
            dma((chunks, rows - 1)),
            dma((chunks, rows - 1)),
            dma((chunks, chips - 1)),
            dma((chunks, chips - 1)),
        ],
        compiler_params=pltpu.CompilerParams(
            collective_id=0, has_side_effects=True, vmem_limit_bytes=60 * 2**20
        ),
        cost_estimate=pl.CostEstimate(
            flops=6 * occupied * cols * depth * width,
            bytes_accessed=4 * chunks * depth * width,
            transcendentals=0,
        ),
        name="ladder_exchange",
    )(amplitudes, integrals)


def solution(mesh):
    rows, cols = mesh.shape["row"], mesh.shape["col"]
    return jax.shard_map(
        functools.partial(body, rows, cols),
        mesh=mesh,
        in_specs=(P("col", "row"), P(("row", "col"), None)),
        out_specs=P("col", "row"),
        check_vma=False,
    )
```

time: 540 us -> 258 us (0.48)
  Pallas kernels: 0 us -> 256 us
  blocking collectives: 192 us -> 0 us
  matrix products: 166 us -> 0 us
  waiting for transfers between devices: 130 us -> 0 us
  local copies, waits for them, and re-layouts: 34.9 us -> 1.77 us
  between operations: 13.4 us -> 0.01 us
    pallas_call x0 -> x1, Pallas kernels: none -> 256 us  [body(): pl.pallas_call(functools.partial(kernel, rows, cols, m, chunks, depth, tn...]
    all_to_all x1 -> x0, blocking collectives: 192 us -> none  [body(): lax.all_to_all(amplitudes, 'col', split_axis=1, concat_axis=0, tiled=True)]
    dot_general x1 -> x0, matrix products: 166 us -> none  [body(): jnp.dot(received, integrals, precision=lax.Precision.HIGHEST, preferred_e...]
    reduce_scatter x2 -> x0, waiting for transfers between devices: 130 us -> none  [the longest x1 92.6 us: body(): lax.psum_scatter(jnp.dot(received, integrals, precision=lax.Precision.HIG...]
    all_to_all x1 -> x0, local copies, waits for them, and re-layouts: 17.5 us -> none  [body(): lax.all_to_all(amplitudes, 'col', split_axis=1, concat_axis=0, tiled=True)]
    unnamed x1, local copies, waits for them, and re-layouts: 17.4 us -> 1.77 us
  transfers between devices with their start and end apart: 2 -> 0, of which waited for: 2 -> 0; matrix products, arithmetic and copies ran while one was open for 0% -> 0% of each run, Pallas kernels for 0% -> 0%
where the time goes in v1:
time: 258 us
  Pallas kernels  256 us (99%)
    pallas_call x1, Pallas kernels, body(): pl.pallas_call(functools.partial(kernel, rows, cols, m, chunks, depth, tn...  256 us

profile of v1, /device:TPU:0, one launch (start us, length us, event | category | flops | bytes accessed | tf_op | source)
XLA Modules:
  0.0 257.5 jit_solution(11100294632505475199)
XLA Ops:
  0.0 255.7 %ladder_exchange.1 = f32[128,768]{1,0:T(8,128)} custom-call(f32[128,32768]{1,0:T(8,128)} %a.1, f32[4096,3072]{1,0:T(8,128)} %b.1), custom_call_target="tpu_custom_call" | custom-call | flops 77309411328 | bytes 201326592 | tf_op jit(solution)/shard_map/ladder_exchange/pallas_call | solution.py:256
  255.7 1.8 copy.4

commit v2 on v1

--- a/solution.py
+++ b/solution.py
@@ -9,21 +9,21 @@
 
 MESH = pl.DeviceIdType.MESH
 BF16, F32 = jnp.bfloat16, jnp.float32
-SLOTS = 3
-CHUNKS = 4
+SLOTS = 5
+CHUNKS = 8
 
 
 def kernel(
     rows, cols, m, chunks, depth, tn, kt,
     a, b, out,
-    recv, xhi, xlo, bbuf, acc, part, pair_in, z_in, plane, plane_in,
+    recv, x, bbuf, acc, part, pair_in, z_in, plane, plane_in,
     own_sem, a_send, a_recv, b_sem, p_send, p_recv, z_send, z_recv, q_send, q_recv,
 ):
     r, c = lax.axis_index("row"), lax.axis_index("col")
     chips = cols // 2
     core, chip = lax.rem(c, 2), lax.div(c, 2)
     sibling = c + 1 - 2 * core
-    half = chips * m
+    half, wide = chips * m, cols * m
     slab = out.shape[1]
     per = slab // tn
     tiles = rows * per
@@ -148,11 +148,10 @@
             block = bbuf[slot, at, :]
             bh = block.astype(BF16)
             bl = (block - bh.astype(F32)).astype(BF16)
-            xh, xl = xhi[:, at], xlo[:, at]
+            both = jnp.dot(x[:, at], bh, preferred_element_type=F32)
             acc[...] += (
-                jnp.dot(xh, bh, preferred_element_type=F32)
-                + jnp.dot(xl, bh, preferred_element_type=F32)
-                + jnp.dot(xh, bl, preferred_element_type=F32)
+                both[:wide] + both[wide:]
+                + jnp.dot(x[:wide, at], bl, preferred_element_type=F32)
             )
 
         now = lax.rem(s, 2)
@@ -210,8 +209,8 @@
             at = pl.ds(pl.multiple_of(kk * kt, 128), kt)
             block = recv[s, :, at]
             high = block.astype(BF16)
-            xhi[:, at] = high
-            xlo[:, at] = (block - high.astype(F32)).astype(BF16)
+            x[:wide, at] = high
+            x[wide:, at] = (block - high.astype(F32)).astype(BF16)
 
         @pl.loop(0, rows)
         def _(jr):
@@ -248,7 +247,7 @@
     chunks = occupied // m
     slab = width // rows
     tn = 256 if slab % 256 == 0 else 128
-    kt = min(512, depth)
+    kt = min(1024, depth)
     chips = cols // 2
     half = chips * m
     dma = pltpu.SemaphoreType.DMA
@@ -260,8 +259,7 @@
         out_specs=pl.BlockSpec(memory_space=vmem),
         scratch_shapes=[
             vmem((chunks, cols * m, depth), F32),
-            vmem((cols * m, depth), BF16),
-            vmem((cols * m, depth), BF16),
+            vmem((2 * cols * m, depth), BF16),
             vmem((SLOTS, depth, tn), F32),
             vmem((cols * m, tn), F32),
             vmem((2, 2, rows, half, slab), F32),

time: 258 us -> 237 us (0.919)
  Pallas kernels: 256 us -> 235 us
    pallas_call x1, Pallas kernels: 256 us -> 235 us  [body(): pl.pallas_call(functools.partial(kernel, rows, cols, m, chunks, depth, tn...]
where the time goes in v2:
time: 237 us
  Pallas kernels  235 us (99%)
    pallas_call x1, Pallas kernels, body(): pl.pallas_call(functools.partial(kernel, rows, cols, m, chunks, depth, tn...  235 us

profile of v2, /device:TPU:0, one launch (start us, length us, event | category | flops | bytes accessed | tf_op | source)
XLA Modules:
  0.0 236.8 jit_solution(14570063359963335876)
XLA Ops:
  0.0 235.0 %ladder_exchange.1 = f32[128,768]{1,0:T(8,128)} custom-call(f32[128,32768]{1,0:T(8,128)} %a.1, f32[4096,3072]{1,0:T(8,128)} %b.1), custom_call_target="tpu_custom_call" | custom-call | flops 77309411328 | bytes 402653184 | tf_op jit(solution)/shard_map/ladder_exchange/pallas_call | solution.py:255
  235.0 1.8 copy.4

commit v3 on v2

--- a/solution.py
+++ b/solution.py
@@ -247,7 +247,7 @@
     chunks = occupied // m
     slab = width // rows
     tn = 256 if slab % 256 == 0 else 128
-    kt = min(1024, depth)
+    kt = min(2048, depth)
     chips = cols // 2
     half = chips * m
     dma = pltpu.SemaphoreType.DMA

time: 237 us -> 233 us (0.983)
  Pallas kernels: 235 us -> 231 us
    pallas_call x1, Pallas kernels: 235 us -> 231 us  [body(): pl.pallas_call(functools.partial(kernel, rows, cols, m, chunks, depth, tn...]
where the time goes in v3:
time: 233 us; the launch traced here: 232 us
  Pallas kernels  231 us (99%)
    pallas_call x1, Pallas kernels, body(): pl.pallas_call(functools.partial(kernel, rows, cols, m, chunks, depth, tn...  231 us

profile of v3, /device:TPU:0, one launch (start us, length us, event | category | flops | bytes accessed | tf_op | source)
XLA Modules:
  0.0 232.5 jit_solution(15768724189099909175)
XLA Ops:
  0.0 230.7 %ladder_exchange.1 = f32[128,768]{1,0:T(8,128)} custom-call(f32[128,32768]{1,0:T(8,128)} %a.1, f32[4096,3072]{1,0:T(8,128)} %b.1), custom_call_target="tpu_custom_call" | custom-call | flops 77309411328 | bytes 402653184 | tf_op jit(solution)/shard_map/ladder_exchange/pallas_call | solution.py:255
  230.7 1.8 copy.4
